TPU v7x, 256 devices: a whole 4x4x8 slice. The times are simulated.
256 devices in a mesh: frame: 4 (over y), space: 64 (over x, z, core).
Axes of the slice: x: 4, y: 4, z: 8, core: 2. Of those that a mesh axis runs over, the one named last changes fastest.
Arguments:
- labels: int32 [128, 128, 512], P('space'), may hold values from 0 to 7
- region_conductivity: float32 [8], replicated, may hold values from 0.3 to 3
- source: float32 [4, 3, 64, 64, 256], P('frame', None, 'space'), may hold values from -9 to 9
- receivers: int32 [4, 3, 256], P('frame'), may hold values from 0 to 511, as said below
- observed: float32 [4, 256], P('frame'), may hold values from -2 to 2
Outputs:
- search_direction: float32 [4, 3, 64, 64, 256], P('frame', None, 'space')
- data_residual: float32 [4, 256], P('frame')
Inputs may be any that keep to these rules, and one draw needn't show every extreme that they name: receivers[f, 0, k] is below 128, receivers[f, 1, k] below 128, receivers[f, 2, k] below 512.
All inputs are finite; a program needn't handle non-finite values.
Results may differ from a plain program's by a relative error of at most 0.0003.
Values sent between devices are 32-bit elements; how exact they have to be, the bound alone decides.
A program may use at most 64 MiB of HBM per device.

v0:
```python
import functools

import jax
import jax.numpy as jnp
import numpy as np
from jax import lax
from jax.experimental import pallas as pl
from jax.experimental.pallas import tpu as pltpu
from jax.sharding import PartitionSpec as P

SMOOTHING = 4.0
PAD = 8
ROWS = 8
PLANES = 7
MESH = pl.DeviceIdType.MESH
F32 = jnp.float32
BF16 = jnp.bfloat16


def smoothing_inverse(frames):
    matrix = np.zeros((frames, frames))
    for f in range(frames):
        near = [g for g in (f - 1, f + 1) if 0 <= g < frames]
        matrix[f, f] = 1.0 + SMOOTHING * len(near)
        for g in near:
            matrix[f, g] = -SMOOTHING
    return np.linalg.inv(matrix)


def parts_of(x):
    high = x.astype(BF16)
    rest = x - high.astype(F32)
    middle = rest.astype(BF16)
    low = (rest - middle.astype(F32)).astype(BF16)
    return high, middle, low


def dot(a, b):
    return jnp.dot(a, b, preferred_element_type=F32)


def lanes_to_sublanes(row):
    n = row.shape[1]
    same = lax.broadcasted_iota(jnp.int32, (n, n), 0) == lax.broadcasted_iota(jnp.int32, (n, n), 1)
    return jnp.sum(jnp.where(same, row, jnp.zeros_like(row)), axis=1, keepdims=True)


def sublanes_to_lanes(column):
    n = column.shape[0]
    same = lax.broadcasted_iota(jnp.int32, (n, n), 0) == lax.broadcasted_iota(jnp.int32, (n, n), 1)
    return jnp.sum(jnp.where(same, column, jnp.zeros_like(column)), axis=0, keepdims=True)


def folded(x):
    total = x[:, :128]
    for start in range(128, x.shape[1], 128):
        total = total + x[:, start : start + 128]
    return total


def cg_coefficients(m):
    m0, m1, m2, m3, m4, m5 = m
    a0 = m0 / m1
    rr1 = m0 - 2.0 * a0 * m1 + a0 * a0 * m2
    b0 = rr1 / m0
    p0, p1 = 1.0 + b0, -a0
    a1 = rr1 / (p0 * p0 * m1 + 2.0 * p0 * p1 * m2 + p1 * p1 * m3)
    r0, r1, r2 = 1.0, -a0 - a1 * p0, -a1 * p1
    rr2 = m0 + r1 * r1 * m2 + r2 * r2 * m4 + 2.0 * (r1 * m1 + r2 * m2 + r1 * r2 * m3)
    b1 = rr2 / rr1
    q0, q1, q2 = r0 + b1 * p0, r1 + b1 * p1, r2
    curv = q0 * q0 * m1 + q1 * q1 * m3 + q2 * q2 * m5
    curv = curv + 2.0 * (q0 * q1 * m2 + q0 * q2 * m3 + q1 * q2 * m4)
    a2 = rr2 / curv
    return a0 + a1 * p0 + a2 * q0, a1 * p1 + a2 * q1, a2 * q2


def kernel(
    frames, slabs, regions,
    labels_ref, cond_ref, source_ref, recv_hbm, obs_hbm,
    out_ref, misfit_ref,
    lab, src, recv_ref, obs_ref, h, v0, v1, v2, diag, kxo, kxm, kyo, kym, kz,
    czb, qs, up, tall, gat, hot_y, msg, got1, got2, pmsg, pgot, dmsg, dgot, wc, wg, uq, uf,
    load_sem, h_send, h_recv, q_send, q_recv, ar_send, ar_recv, p_send, p_recv, y_send, y_recv, known,
):
    nx, ny = lab.shape[1], lab.shape[2]
    nxc, nyc = nx // 2, ny // 2
    recv = recv_ref.shape[1]
    quarter = nxc // frames
    chunks = nx // ROWS
    f = lax.axis_index("frame")
    s = lax.axis_index("space")

    def slab_at(by):
        return lax.rem(s + by + slabs, slabs)

    def frame_at(by):
        return lax.rem(f + by, frames)

    barrier = pltpu.get_barrier_semaphore()

    def tell(semaphore, slabs_by, others):
        for by in slabs_by:
            pl.semaphore_signal(semaphore, inc=1, device_id=(f, slab_at(by)), device_id_type=MESH)
        if others:
            for k in range(1, frames):
                pl.semaphore_signal(semaphore, inc=1, device_id=(frame_at(k), s), device_id_type=MESH)
        return len(slabs_by) + (frames - 1 if others else 0)

    reach = slabs // 16
    quarters = [slabs // 4, slabs // 2, slabs - slabs // 4]
    near = [by for k in range(1, reach + 1) for by in (k, -k)]
    greeted = tell(barrier, near + quarters, True)

    load_labels = pltpu.make_async_copy(labels_ref, lab, load_sem.at[0])
    load_source = pltpu.make_async_copy(source_ref.at[0, :, 0], src, load_sem.at[1])
    load_labels.start()
    load_source.start()
    load_recv = pltpu.make_async_copy(recv_hbm.at[:, 0], recv_ref, load_sem.at[2])
    load_obs = pltpu.make_async_copy(obs_hbm, obs_ref, load_sem.at[3])
    load_recv.start()
    load_obs.start()

    load_labels.wait()

    def convert(i, carry):
        p, r = i // chunks, i % chunks
        here = lab[p, pl.ds(pl.multiple_of(r * ROWS, ROWS), ROWS), :]
        value = jnp.full((ROWS, ny), 0.5 * cond_ref[0], F32)
        for region in range(1, regions):
            value = jnp.where(here == region, 0.5 * cond_ref[region], value)
        h[p + 2, pl.ds(pl.multiple_of(PAD + r * ROWS, ROWS), ROWS), :] = value
        return carry

    lax.fori_loop(0, 2 * chunks, convert, 0, unroll=chunks)
    load_source.wait()

    pl.semaphore_wait(barrier, greeted)
    heard = tell(known.at[0], [reach, -reach], True)

    def remote(src_ref, dst_ref, sems, index, device):
        return pltpu.make_async_remote_copy(
            src_ref=src_ref, dst_ref=dst_ref, send_sem=sems[0].at[index], recv_sem=sems[1].at[index],
            device_id=device, device_id_type=MESH,
        )

    def send(*args):
        copy = remote(*args)
        copy.start()
        return copy

    def plane(p):
        return h.at[p, pl.ds(PAD, nx), :]

    def strip(p):
        rows = nx // frames
        return h.at[p, pl.ds(pl.multiple_of(PAD + f * rows, ROWS), rows), :]

    copy_cz = send(src.at[0], czb, (q_send, q_recv), 0, (f, slab_at(1)))
    h_sems = (h_send, h_recv)
    odd = lax.rem(s, 2) == 1
    copy_strip = remote(strip(2), strip(6), h_sems, 4, (f, slab_at(-2)))
    copies_strip = [remote(strip(6), strip(6), h_sems, 5 + k, (frame_at(k), s)) for k in range(1, frames)]
    copy_relay = remote(plane(4), plane(6), h_sems, 5, (f, slab_at(-1)))
    pl.when(odd)(copy_strip.start)
    copy_h1 = send(plane(3), plane(1), h_sems, 0, (f, slab_at(1)))
    copy_h4 = send(plane(2), plane(4), h_sems, 1, (f, slab_at(-1)))
    copy_h0 = send(plane(2), plane(0), h_sems, 2, (f, slab_at(1)))
    copy_h5 = send(plane(3), plane(5), h_sems, 3, (f, slab_at(-1)))

    row_c = lax.broadcasted_iota(jnp.int32, (nxc, nyc), 0)
    lane_c = lax.broadcasted_iota(jnp.int32, (nxc, nyc), 1)
    along_x, along_y = src[1], src[2]
    total = src[0] + along_x - jnp.where(row_c > 0, pltpu.roll(along_x, 1, 0), 0.0)
    total = total + along_y - jnp.where(lane_c > 0, pltpu.roll(along_y, 1, 1), 0.0)
    copy_cz.wait_recv()
    qs[1] = total - jnp.where(s > 0, czb[...], 0.0)
    q_sems = (q_send, q_recv)
    copies_q = [
        send(qs.at[1], qs.at[0], q_sems, 1, (f, slab_at(1))),
        send(qs.at[1], qs.at[2], q_sems, 2, (f, slab_at(-1))),
        send(qs.at[1], qs.at[3], q_sems, 3, (f, slab_at(-2))),
    ]

    zero_rows = jnp.zeros((PAD, ny), F32)
    for field in (h, v0, v1, v2):
        for p in range(PLANES):
            field[p, 0:PAD, :] = zero_rows
            field[p, PAD + nx : PAD + nx + PAD, :] = zero_rows
    load_recv.wait()
    load_obs.wait()
    first = 2 * s - 2
    zx_row = (recv_ref[0:1, :] - first) * nx + recv_ref[1:2, :]
    zx_col = lanes_to_sublanes(zx_row)
    y_col = lanes_to_sublanes(recv_ref[2:3, :])
    own_ids = lax.broadcasted_iota(jnp.int32, (recv, 2 * nx), 1) + 2 * nx
    gat[...] = (zx_col == own_ids).astype(BF16)
    hot_y[...] = (y_col == lax.broadcasted_iota(jnp.int32, (recv, ny), 1)).astype(BF16)
    coarse_id = lax.broadcasted_iota(jnp.int32, (nyc, ny), 0)
    up[...] = (coarse_id == lax.broadcasted_iota(jnp.int32, (nyc, ny), 1) // 2).astype(BF16)
    z_in = recv_ref[0:1, :] - 2 * s
    inside = (z_in >= 0) & (z_in < 2)

    def valid(p):
        z = first + p
        return (z >= 0) & (z < 2 * slabs)

    def aligned(r):
        return pl.ds(pl.multiple_of(PAD + r * ROWS, ROWS), ROWS)

    def next_row(field, p, r, here):
        return pltpu.roll(jnp.where(sub == 0, field[p, aligned(r + 1), :], here), ROWS - 1, 0)

    def previous_row(field, p, r, here):
        return pltpu.roll(jnp.where(sub == ROWS - 1, field[p, aligned(r - 1), :], here), 1, 0)

    def prolong(c):
        z = s - 1 + c
        ok = (z >= 0) & (z < slabs)
        high, middle, low = parts_of(jnp.where(ok, qs[c], 0.0))
        fine = dot(high, up[...]) + dot(middle, up[...]) + dot(low, up[...])
        for t in range(ny // 128):
            tall[t, pl.ds(0, nxc, 2), :] = fine[:, t * 128 : t * 128 + 128]
            tall[t, pl.ds(1, nxc, 2), :] = fine[:, t * 128 : t * 128 + 128]
        for p in (2 * c, 2 * c + 1):
            if p < PLANES:
                for t in range(ny // 128):
                    v0[p, PAD : PAD + nx, t * 128 : t * 128 + 128] = tall[t]

    lane = lax.broadcasted_iota(jnp.int32, (ROWS, ny), 1)
    sub = lax.broadcasted_iota(jnp.int32, (ROWS, ny), 0)

    def zero_outside(p):
        @pl.when(jnp.logical_not(valid(p)))
        def _():
            h[p, PAD : PAD + nx, :] = jnp.zeros((nx, ny), F32)

    def vertical(e):
        keep = jnp.where(valid(e) & valid(e + 1), 1.0, 0.0).astype(F32)

        def body(r, carry):
            kz[e, pl.ds(pl.multiple_of(r * ROWS, ROWS), ROWS), :] = keep * (h[e, aligned(r), :] + h[e + 1, aligned(r), :])
            return carry

        lax.fori_loop(0, chunks, body, 0, unroll=chunks)

    def coefficients(p):
        def body(r, carry):
            at = pl.ds(pl.multiple_of(r * ROWS, ROWS), ROWS)
            here = h[p, aligned(r), :]
            x_next, x_prev = next_row(h, p, r, here), previous_row(h, p, r, here)
            y_next = jnp.where(lane < ny - 1, pltpu.roll(here, ny - 1, 1), 0.0)
            y_prev = jnp.where(lane > 0, pltpu.roll(here, 1, 1), 0.0)
            kxo[p, at, :] = here + x_next
            kxm[p, at, :] = here + x_prev
            kyo[p, at, :] = jnp.where(lane < ny - 1, here + y_next, 0.0)
            kym[p, at, :] = jnp.where(lane > 0, here + y_prev, 0.0)
            near = x_next + x_prev + y_next + y_prev
            diag[p, at, :] = 6.0 * here + near + h[p - 1, aligned(r), :] + h[p + 1, aligned(r), :]
            return carry

        lax.fori_loop(0, chunks, body, 0, unroll=chunks)

    def operate(src_v, dst_v, p, with_moments, sums):
        def body(r, carry):
            at = pl.ds(pl.multiple_of(r * ROWS, ROWS), ROWS)
            here = src_v[p, aligned(r), :]
            value = diag[p, at, :] * here
            value = value - kxo[p, at, :] * next_row(src_v, p, r, here)
            value = value - kxm[p, at, :] * previous_row(src_v, p, r, here)
            value = value - kyo[p, at, :] * pltpu.roll(here, ny - 1, 1)
            value = value - kym[p, at, :] * pltpu.roll(here, 1, 1)
            value = value - kz[p, at, :] * src_v[p + 1, aligned(r), :]
            value = value - kz[p - 1, at, :] * src_v[p - 1, aligned(r), :]
            dst_v[p, aligned(r), :] = value
            if not with_moments:
                return carry
            return (carry[0] + folded(here * value), carry[1] + folded(value * value))

        return lax.fori_loop(0, chunks, body, sums, unroll=chunks)

    def square(src_v, p, total):
        def body(r, carry):
            here = src_v[p, aligned(r), :]
            return carry + folded(here * here)

        return lax.fori_loop(0, chunks, body, total, unroll=chunks)

    def energy(field, p, total):
        def body(r, carry):
            at = pl.ds(pl.multiple_of(r * ROWS, ROWS), ROWS)
            here = field[p, aligned(r), :]
            near = kxo[p, at, :] * next_row(field, p, r, here)
            near = near + kyo[p, at, :] * pltpu.roll(here, ny - 1, 1)
            near = near + kz[p, at, :] * field[p + 1, aligned(r), :]
            return carry + folded(here * (diag[p, at, :] * here - 2.0 * near))

        return lax.fori_loop(0, chunks, body, total, unroll=chunks)

    nothing = jnp.zeros((ROWS, 128), F32)

    def krylov_own():
        m0 = square(v0, 3, square(v0, 2, nothing))
        return m0, operate(v0, v1, 3, True, operate(v0, v1, 2, True, (nothing, nothing)))

    def krylov_near():
        for p in (1, 4):
            operate(v0, v1, p, False, 0)
        m34 = operate(v1, v2, 3, True, operate(v1, v2, 2, True, (nothing, nothing)))
        return m34, energy(v2, 2, nothing)

    def krylov_far(m5):
        operate(v0, v1, 5, False, 0)
        operate(v1, v2, 4, False, 0)
        return energy(v2, 3, m5)

    def summed(*moments):
        place = lax.broadcasted_iota(jnp.int32, (1, 128), 1)
        row = jnp.zeros((1, 128), F32)
        for j, m in enumerate(moments):
            row = jnp.where(place == j, jnp.sum(jnp.sum(m, axis=0, keepdims=True), axis=1, keepdims=True), row)
        return row

    def share(source, landing, index):
        def start(i, carry):
            k = lax.rem(i + slabs // 2, slabs - 1) + 1
            pltpu.make_async_remote_copy(
                src_ref=source, dst_ref=landing.at[s], send_sem=ar_send.at[index], recv_sem=ar_recv.at[index],
                device_id=(f, slab_at(k)), device_id_type=MESH,
            ).start()
            return carry

        lax.fori_loop(0, slabs - 1, start, 0)

    def shared(landing, index):
        others = landing.at[pl.ds(0, slabs - 1)]
        whole = pltpu.make_async_remote_copy(
            src_ref=others, dst_ref=others, send_sem=ar_send.at[index], recv_sem=ar_recv.at[index],
            device_id=(f, slab_at(1)), device_id_type=MESH,
        )
        whole.wait_send()
        whole.wait_recv()

    def moments_of(landing):
        total = jnp.sum(landing[...], axis=0)
        return [total[:, j : j + 1] for j in range(6)]

    @pl.when(odd)
    def _():
        copy_strip.wait_recv()
        for copy in copies_strip:
            copy.start()

    copy_h1.wait_recv()
    copy_h4.wait_recv()
    zero_outside(1)
    zero_outside(4)
    pl.when(odd)(copy_relay.start)
    for e in (1, 2, 3):
        vertical(e)
    for p in (2, 3):
        coefficients(p)
    for copy in copies_q:
        copy.wait_recv()
    for c in range(4):
        prolong(c)
    m0, m12 = krylov_own()
    pl.semaphore_wait(known.at[0], heard)
    heard = tell(known.at[1], quarters, False)
    copy_h0.wait_recv()
    copy_h5.wait_recv()
    zero_outside(0)
    zero_outside(5)
    vertical(0)
    vertical(4)
    coefficients(1)
    coefficients(4)
    m34, m5 = krylov_near()

    @pl.when(odd)
    def _():
        for copy in copies_strip:
            copy.wait()

    pl.when(jnp.logical_not(odd))(copy_relay.wait_recv)
    zero_outside(6)
    vertical(5)
    coefficients(5)
    m5 = krylov_far(m5)
    moments = summed(m0, *m12, *m34, m5)
    msg[0] = moments
    got1[s] = moments
    pl.semaphore_wait(known.at[1], heard)
    share(msg.at[0], got1, 0)

    for j, field in enumerate((v0, v1, v2)):
        whole = jnp.concatenate([field[2, PAD : PAD + nx, :], field[3, PAD : PAD + nx, :]], axis=0)
        rows = sum(dot(gat[...], part) for part in parts_of(whole))
        column = jnp.sum(rows * hot_y[...].astype(F32), axis=1, keepdims=True)
        pmsg[j] = sublanes_to_lanes(column)
    p_sems = (p_send, p_recv)
    copies_p = [
        send(pmsg, pgot.at[0], p_sems, 0, (f, slab_at(1))),
        send(pmsg, pgot.at[1], p_sems, 1, (f, slab_at(-1))),
        send(pmsg, pgot.at[2], p_sems, 2, (f, slab_at(-2))),
    ]
    shared(got1, 0)
    c0, c1, c2 = cg_coefficients(moments_of(got1))
    observed = obs_ref[...]

    def misfit(values):
        return c0 * values[0] + c1 * values[1] + c2 * values[2] - observed

    mine = jnp.where(inside, misfit([pmsg[j] for j in range(3)]), 0.0)
    dmsg[...] = mine
    dgot[s] = mine
    share(dmsg, dgot, 1)
    for copy in copies_p:
        copy.wait_recv()
    d = misfit([pmsg[j] + pgot[0, j] + pgot[1, j] + pgot[2, j] for j in range(3)])

    d_parts = parts_of(d)
    for p in range(PLANES):
        hit = zx_row == lax.broadcasted_iota(jnp.int32, (nx, recv), 0) + p * nx
        value = sum(dot(jnp.where(hit, part.astype(F32), 0.0).astype(BF16), hot_y[...]) for part in d_parts)
        v0[p, PAD : PAD + nx, :] = jnp.where(valid(p), value, 0.0)
    m0, m12 = krylov_own()
    m34, m5 = krylov_near()
    moments = summed(m0, *m12, *m34, krylov_far(m5))
    msg[1] = moments
    got2[s] = moments
    share(msg.at[1], got2, 2)
    shared(got2, 2)
    c0, c1, c2 = cg_coefficients(moments_of(got2))

    def restrict(r, carry):
        at = aligned(r)
        fine = [c0 * v0[p, at, :] + c1 * v1[p, at, :] + c2 * v2[p, at, :] for p in (2, 3)]
        both = fine[0] + fine[1]
        for t in range(ny // 128):
            tall[t, pl.ds(pl.multiple_of(r * ROWS, ROWS), ROWS), :] = both[:, t * 128 : t * 128 + 128]
        return carry

    lax.fori_loop(0, chunks, restrict, 0, unroll=chunks)
    pairs = jnp.concatenate(
        [tall[t, pl.ds(0, nxc, 2), :] + tall[t, pl.ds(1, nxc, 2), :] for t in range(ny // 128)], axis=1
    )
    down = (((1,), (1,)), ((), ()))
    wc[...] = sum(lax.dot_general(part, up[...], down, preferred_element_type=F32) for part in parts_of(pairs))

    def part_at(g):
        return pl.ds(pl.multiple_of(g * quarter, quarter), quarter)

    wg[f] = wc[part_at(f), :]
    y_sems = (y_send, y_recv)
    copies_w = [
        send(wc.at[part_at(frame_at(k)), :], wg.at[f], y_sems, k - 1, (frame_at(k), s)) for k in range(1, frames)
    ]
    for copy in copies_w:
        copy.wait_recv()
    inverse = smoothing_inverse(frames)
    for g in range(frames):
        uq[g] = sum(float(inverse[g, k]) * wg[k] for k in range(frames))
    uf[0, part_at(f), :] = uq[f]
    copies_u = []
    for k in range(frames):
        to = frame_at(k)
        copies_u.append(send(uq.at[to], uf.at[1, part_at(f), :], y_sems, 2 * frames + k, (to, slab_at(-1))))
        if k > 0:
            copies_u.append(send(uq.at[to], uf.at[0, part_at(f), :], y_sems, frames + k, (to, s)))
    shared(dgot, 1)
    misfit_ref[...] = jnp.sum(dgot[...], axis=0)
    for copy in copies_u:
        copy.wait_recv()
    u = uf[0]
    out_ref[0] = u - jnp.where(s < slabs - 1, uf[1], 0.0)
    out_ref[1] = u - jnp.where(row_c < nxc - 1, pltpu.roll(u, nxc - 1, 0), 0.0)
    out_ref[2] = u - jnp.where(lane_c < nyc - 1, pltpu.roll(u, nyc - 1, 1), 0.0)
    @pl.when(odd)
    def _():
        for copy in [copy_strip, copy_relay]:
            copy.wait_send()

    for copy in [copy_cz, copy_h0, copy_h1, copy_h4, copy_h5, *copies_q, *copies_p, *copies_w, *copies_u]:
        copy.wait_send()


def shards(frames, slabs, labels, region_conductivity, source, receivers, observed):
    _, nx, ny = labels.shape
    nxc, nyc = nx // 2, ny // 2
    recv = receivers.shape[2]
    quarter = nxc // frames
    vmem = pl.BlockSpec(memory_space=pltpu.VMEM)
    hbm = pl.BlockSpec(memory_space=pltpu.HBM)
    plane = (PLANES, nx, ny)
    padded = (PLANES, nx + 2 * PAD, ny)
    scratch = [
        pltpu.VMEM((2, nx, ny), jnp.int32),
        pltpu.VMEM((3, nxc, nyc), F32),
        pltpu.VMEM((3, recv), jnp.int32),
        pltpu.VMEM((1, recv), F32),
        *[pltpu.VMEM(padded, F32) for _ in range(4)],
        *[pltpu.VMEM(plane, F32) for _ in range(6)],
        pltpu.VMEM((nxc, nyc), F32),
        pltpu.VMEM((4, nxc, nyc), F32),
        pltpu.VMEM((nyc, ny), BF16),
        pltpu.VMEM((ny // 128, nx, 128), F32),
        pltpu.VMEM((recv, 2 * nx), BF16),
        pltpu.VMEM((recv, ny), BF16),
        pltpu.VMEM((2, 1, 128), F32),
        pltpu.VMEM((slabs, 1, 128), F32),
        pltpu.VMEM((slabs, 1, 128), F32),
        pltpu.VMEM((3, 1, recv), F32),
        pltpu.VMEM((3, 3, 1, recv), F32),
        pltpu.VMEM((1, recv), F32),
        pltpu.VMEM((slabs, 1, recv), F32),
        pltpu.VMEM((nxc, nyc), F32),
        pltpu.VMEM((frames, quarter, nyc), F32),
        pltpu.VMEM((frames, quarter, nyc), F32),
        pltpu.VMEM((2, nxc, nyc), F32),
        pltpu.SemaphoreType.DMA((4,)),
        *[pltpu.SemaphoreType.DMA((5 + frames,)) for _ in range(2)],
        *[pltpu.SemaphoreType.DMA((4,)) for _ in range(2)],
        *[pltpu.SemaphoreType.DMA((3,)) for _ in range(2)],
        *[pltpu.SemaphoreType.DMA((3,)) for _ in range(2)],
        *[pltpu.SemaphoreType.DMA((3 * frames,)) for _ in range(2)],
        pltpu.SemaphoreType.REGULAR((2,)),
    ]
    out, misfit = pl.pallas_call(
        functools.partial(kernel, frames, slabs, region_conductivity.shape[0]),
        out_shape=(jax.ShapeDtypeStruct((3, nxc, nyc), F32), jax.ShapeDtypeStruct((1, recv), F32)),
        in_specs=[hbm, pl.BlockSpec(memory_space=pltpu.SMEM), hbm, hbm, hbm],
        out_specs=(vmem, vmem),
        scratch_shapes=scratch,
        compiler_params=pltpu.CompilerParams(
            collective_id=0, has_side_effects=True, vmem_limit_bytes=64 * 1024 * 1024
        ),
    )(labels, region_conductivity, source, jnp.transpose(receivers, (1, 0, 2)), observed)
    return out.reshape(1, 3, 1, nxc, nyc), misfit


def solution(mesh):
    in_specs = (
        P("space", None, None),
        P(),
        P("frame", None, "space", None, None),
        P("frame", None, None),
        P("frame", None),
    )
    out_specs = (P("frame", None, "space", None, None), P("frame", None))
    body = functools.partial(shards, mesh.shape["frame"], mesh.shape["space"])
    return jax.shard_map(body, mesh=mesh, in_specs=in_specs, out_specs=out_specs, check_vma=False)
```

profile of v0, /device:TPU:1, one launch (start us, length us, event | category | flops | bytes accessed | tf_op | source)
XLA Modules:
  0.0 54.9 jit_solution(15246254942207821526)
XLA Ops:
  0.6 52.1 %shard_map.68 = (f32[3,64,256]{2,1,0:T(8,128)}, f32[1,256]{1,0:T(1,128)}) custom-call(s32[2,128,512]{2,1,0:T(8,128)} %labels_ref.1, f32[8]{0:T(128)} %cond_ref.1, f32[1,3,1,64,256]{4,3,2,1,0:T(8,128)} %source_ref.1, s32[3,1,256]{2,1,0:T(1,128)} %bitcast.5, f32[1,256]{1,0:T(1,128)} %obs_hbm.1), custom_call_target="tpu_custom_call" | custom-call | tf_op jit(solution)/shard_map/pallas_call | solution.py:529
  52.7 0.0 copy-start
  52.7 1.6 %copy.10 = f32[1,3,1,64,256]{4,3,2,1,0:T(8,128)} copy(f32[1,3,1,64,256]{4,3,2,1,0:T(8,128)} %bitcast.4) | data formatting | bytes 393216
  54.4 0.0 copy-done
  54.4 0.6 %copy.11 = f32[1,256]{1,0:T(1,128)} copy(f32[1,256]{1,0:T(1,128)S(1)} %copy-done) | data formatting | bytes 2048
Async XLA Ops:
  52.7 1.6 %copy-start = (f32[1,256]{1,0:T(1,128)S(1)}, f32[1,256]{1,0:T(1,128)}, u32[]{:S(2)}) copy-start(f32[1,256]{1,0:T(1,128)} %get-tuple-element.11) | copy-start | bytes 3076
where the time goes:
time: 55 us; the launch traced here: 54.9 us
  Pallas kernels  52.1 us (95%)
  local copies, waits for them, and re-layouts  2.18 us (4%)
  between operations  0.65 us (1%)
    pallas_call x1, Pallas kernels, shards(): pl.pallas_call(functools.partial(kernel, frames, slabs, region_conductivi...  52.1 us
    unnamed x4, local copies, waits for them, and re-layouts  2.18 us

commit v1 on v0

--- a/solution.py
+++ b/solution.py
@@ -80,7 +80,7 @@
     labels_ref, cond_ref, source_ref, recv_hbm, obs_hbm,
     out_ref, misfit_ref,
     lab, src, recv_ref, obs_ref, h, v0, v1, v2, diag, kxo, kxm, kyo, kym, kz,
-    czb, qs, up, tall, gat, hot_y, msg, got1, got2, pmsg, pgot, dmsg, dgot, wc, wg, uq, uf,
+    czb, qs, up, tall, gat, hot_y, msg, got1, got2, pmsg, pgot, dmsg, dgot, wq, wg, cmsg, cgot, uq, uf,
     load_sem, h_send, h_recv, q_send, q_recv, ar_send, ar_recv, p_send, p_recv, y_send, y_recv, known,
 ):
     nx, ny = lab.shape[1], lab.shape[2]
@@ -165,8 +165,6 @@
     pl.when(odd)(copy_strip.start)
     copy_h1 = send(plane(3), plane(1), h_sems, 0, (f, slab_at(1)))
     copy_h4 = send(plane(2), plane(4), h_sems, 1, (f, slab_at(-1)))
-    copy_h0 = send(plane(2), plane(0), h_sems, 2, (f, slab_at(1)))
-    copy_h5 = send(plane(3), plane(5), h_sems, 3, (f, slab_at(-1)))
 
     row_c = lax.broadcasted_iota(jnp.int32, (nxc, nyc), 0)
     lane_c = lax.broadcasted_iota(jnp.int32, (nxc, nyc), 1)
@@ -179,9 +177,13 @@
     copies_q = [
         send(qs.at[1], qs.at[0], q_sems, 1, (f, slab_at(1))),
         send(qs.at[1], qs.at[2], q_sems, 2, (f, slab_at(-1))),
-        send(qs.at[1], qs.at[3], q_sems, 3, (f, slab_at(-2))),
     ]
-
+    copy_q3 = remote(qs.at[1], qs.at[3], q_sems, 3, (f, slab_at(-2)))
+    relay_q3 = remote(qs.at[2], qs.at[3], q_sems, 4, (f, slab_at(-1)))
+    pl.when(odd)(copy_q3.start)
+
+    copy_h0 = send(plane(2), plane(0), h_sems, 2, (f, slab_at(1)))
+    copy_h5 = send(plane(3), plane(5), h_sems, 3, (f, slab_at(-1)))
     zero_rows = jnp.zeros((PAD, ny), F32)
     for field in (h, v0, v1, v2):
         for p in range(PLANES):
@@ -362,7 +364,8 @@
         coefficients(p)
     for copy in copies_q:
         copy.wait_recv()
-    for c in range(4):
+    pl.when(odd)(relay_q3.start)
+    for c in range(3):
         prolong(c)
     m0, m12 = krylov_own()
     pl.semaphore_wait(known.at[0], heard)
@@ -379,10 +382,16 @@
 
     @pl.when(odd)
     def _():
+        copy_q3.wait_recv()
         for copy in copies_strip:
             copy.wait()
 
-    pl.when(jnp.logical_not(odd))(copy_relay.wait_recv)
+    @pl.when(jnp.logical_not(odd))
+    def _():
+        relay_q3.wait_recv()
+        copy_relay.wait_recv()
+
+    prolong(3)
     zero_outside(6)
     vertical(5)
     coefficients(5)
@@ -430,58 +439,60 @@
     msg[1] = moments
     got2[s] = moments
     share(msg.at[1], got2, 2)
+    down = (((1,), (1,)), ((), ()))
+    for j, field in enumerate((v0, v1, v2)):
+        for t in range(ny // 128):
+            at = slice(t * 128, t * 128 + 128)
+            tall[t] = field[2, PAD : PAD + nx, at] + field[3, PAD : PAD + nx, at]
+        pairs = jnp.concatenate(
+            [tall[t, pl.ds(0, nxc, 2), :] + tall[t, pl.ds(1, nxc, 2), :] for t in range(ny // 128)], axis=1
+        )
+        coarse = sum(lax.dot_general(part, up[...], down, preferred_element_type=F32) for part in parts_of(pairs))
+        for g in range(frames):
+            wq[g, j] = coarse[g * quarter : (g + 1) * quarter]
+    y_sems = (y_send, y_recv)
+    wg[0, f] = wq[f]
+    copies_w = [send(wq.at[f], wg.at[1, f], y_sems, 0, (f, slab_at(-1)))]
+    for k in range(1, frames):
+        to = frame_at(k)
+        copies_w.append(send(wq.at[to], wg.at[1, f], y_sems, k, (to, slab_at(-1))))
+        copies_w.append(send(wq.at[to], wg.at[0, f], y_sems, frames + k, (to, s)))
     shared(got2, 2)
-    c0, c1, c2 = cg_coefficients(moments_of(got2))
-
-    def restrict(r, carry):
-        at = aligned(r)
-        fine = [c0 * v0[p, at, :] + c1 * v1[p, at, :] + c2 * v2[p, at, :] for p in (2, 3)]
-        both = fine[0] + fine[1]
-        for t in range(ny // 128):
-            tall[t, pl.ds(pl.multiple_of(r * ROWS, ROWS), ROWS), :] = both[:, t * 128 : t * 128 + 128]
-        return carry
-
-    lax.fori_loop(0, chunks, restrict, 0, unroll=chunks)
-    pairs = jnp.concatenate(
-        [tall[t, pl.ds(0, nxc, 2), :] + tall[t, pl.ds(1, nxc, 2), :] for t in range(ny // 128)], axis=1
-    )
-    down = (((1,), (1,)), ((), ()))
-    wc[...] = sum(lax.dot_general(part, up[...], down, preferred_element_type=F32) for part in parts_of(pairs))
-
-    def part_at(g):
-        return pl.ds(pl.multiple_of(g * quarter, quarter), quarter)
-
-    wg[f] = wc[part_at(f), :]
-    y_sems = (y_send, y_recv)
-    copies_w = [
-        send(wc.at[part_at(frame_at(k)), :], wg.at[f], y_sems, k - 1, (frame_at(k), s)) for k in range(1, frames)
-    ]
+    place = lax.broadcasted_iota(jnp.int32, (1, 128), 1)
+    c_row = jnp.zeros((1, 128), F32)
+    for j, c in enumerate(cg_coefficients(moments_of(got2))):
+        c_row = jnp.where(place == j, c, c_row)
+    cmsg[...] = c_row
+    cgot[f] = c_row
+    copies_c = [send(cmsg, cgot.at[f], y_sems, 2 * frames + k, (frame_at(k), s)) for k in range(1, frames)]
+
     for copy in copies_w:
         copy.wait_recv()
+    for copy in copies_c:
+        copy.wait_recv()
     inverse = smoothing_inverse(frames)
-    for g in range(frames):
-        uq[g] = sum(float(inverse[g, k]) * wg[k] for k in range(frames))
-    uf[0, part_at(f), :] = uq[f]
-    copies_u = []
-    for k in range(frames):
-        to = frame_at(k)
-        copies_u.append(send(uq.at[to], uf.at[1, part_at(f), :], y_sems, 2 * frames + k, (to, slab_at(-1))))
-        if k > 0:
-            copies_u.append(send(uq.at[to], uf.at[0, part_at(f), :], y_sems, frames + k, (to, s)))
+    for side in range(2):
+        w = [sum(cgot[k][:, j : j + 1] * wg[side, k, j] for j in range(3)) for k in range(frames)]
+        for g in range(frames):
+            uq[g, side] = sum(float(inverse[g, k]) * w[k] for k in range(frames))
+    uf[f] = uq[f]
+    copies_u = [send(uq.at[frame_at(k)], uf.at[f], y_sems, 3 * frames + k, (frame_at(k), s)) for k in range(1, frames)]
     shared(dgot, 1)
     misfit_ref[...] = jnp.sum(dgot[...], axis=0)
     for copy in copies_u:
         copy.wait_recv()
-    u = uf[0]
-    out_ref[0] = u - jnp.where(s < slabs - 1, uf[1], 0.0)
+    u = jnp.concatenate([uf[g, 0] for g in range(frames)], axis=0)
+    above = jnp.concatenate([uf[g, 1] for g in range(frames)], axis=0)
+    out_ref[0] = u - jnp.where(s < slabs - 1, above, 0.0)
     out_ref[1] = u - jnp.where(row_c < nxc - 1, pltpu.roll(u, nxc - 1, 0), 0.0)
     out_ref[2] = u - jnp.where(lane_c < nyc - 1, pltpu.roll(u, nyc - 1, 1), 0.0)
+
     @pl.when(odd)
     def _():
-        for copy in [copy_strip, copy_relay]:
+        for copy in [copy_strip, copy_relay, copy_q3, relay_q3]:
             copy.wait_send()
 
-    for copy in [copy_cz, copy_h0, copy_h1, copy_h4, copy_h5, *copies_q, *copies_p, *copies_w, *copies_u]:
+    for copy in [copy_cz, copy_h0, copy_h1, copy_h4, copy_h5, *copies_q, *copies_p, *copies_w, *copies_c, *copies_u]:
         copy.wait_send()
 
 
@@ -514,16 +525,18 @@
         pltpu.VMEM((3, 3, 1, recv), F32),
         pltpu.VMEM((1, recv), F32),
         pltpu.VMEM((slabs, 1, recv), F32),
-        pltpu.VMEM((nxc, nyc), F32),
-        pltpu.VMEM((frames, quarter, nyc), F32),
-        pltpu.VMEM((frames, quarter, nyc), F32),
-        pltpu.VMEM((2, nxc, nyc), F32),
+        pltpu.VMEM((frames, 3, quarter, nyc), F32),
+        pltpu.VMEM((2, frames, 3, quarter, nyc), F32),
+        pltpu.VMEM((1, 128), F32),
+        pltpu.VMEM((frames, 1, 128), F32),
+        pltpu.VMEM((frames, 2, quarter, nyc), F32),
+        pltpu.VMEM((frames, 2, quarter, nyc), F32),
         pltpu.SemaphoreType.DMA((4,)),
         *[pltpu.SemaphoreType.DMA((5 + frames,)) for _ in range(2)],
-        *[pltpu.SemaphoreType.DMA((4,)) for _ in range(2)],
+        *[pltpu.SemaphoreType.DMA((5,)) for _ in range(2)],
         *[pltpu.SemaphoreType.DMA((3,)) for _ in range(2)],
         *[pltpu.SemaphoreType.DMA((3,)) for _ in range(2)],
-        *[pltpu.SemaphoreType.DMA((3 * frames,)) for _ in range(2)],
+        *[pltpu.SemaphoreType.DMA((4 * frames,)) for _ in range(2)],
         pltpu.SemaphoreType.REGULAR((2,)),
     ]
     out, misfit = pl.pallas_call(

time: 55 us -> 51.1 us (0.929); the launches traced: 54.9 us -> 50.1 us
  Pallas kernels: 52.1 us -> 47.3 us
    pallas_call x1, Pallas kernels: 52.1 us -> 47.3 us  [shards(): pl.pallas_call(functools.partial(kernel, frames, slabs, region_conductivi...]
where the time goes in v1:
time: 51.1 us; the launch traced here: 50.1 us
  Pallas kernels  47.3 us (93%)
  local copies, waits for them, and re-layouts  2.18 us (4%)
  between operations  0.65 us (1%)
    pallas_call x1, Pallas kernels, shards(): pl.pallas_call(functools.partial(kernel, frames, slabs, region_conductivi...  47.3 us
    unnamed x4, local copies, waits for them, and re-layouts  2.18 us

profile of v1, /device:TPU:1, one launch (start us, length us, event | category | flops | bytes accessed | tf_op | source)
XLA Modules:
  0.0 50.1 jit_solution(4253747420612318513)
XLA Ops:
  0.6 47.3 %shard_map.68 = (f32[3,64,256]{2,1,0:T(8,128)}, f32[1,256]{1,0:T(1,128)}) custom-call(s32[2,128,512]{2,1,0:T(8,128)} %labels_ref.1, f32[8]{0:T(128)} %cond_ref.1, f32[1,3,1,64,256]{4,3,2,1,0:T(8,128)} %source_ref.1, s32[3,1,256]{2,1,0:T(1,128)} %bitcast.5, f32[1,256]{1,0:T(1,128)} %obs_hbm.1), custom_call_target="tpu_custom_call" | custom-call | tf_op jit(solution)/shard_map/pallas_call | solution.py:542
  47.9 0.0 copy-start
  47.9 1.6 %copy.10 = f32[1,3,1,64,256]{4,3,2,1,0:T(8,128)} copy(f32[1,3,1,64,256]{4,3,2,1,0:T(8,128)} %bitcast.4) | data formatting | bytes 393216
  49.5 0.0 copy-done
  49.5 0.6 %copy.11 = f32[1,256]{1,0:T(1,128)} copy(f32[1,256]{1,0:T(1,128)S(1)} %copy-done) | data formatting | bytes 2048
Async XLA Ops:
  47.9 1.6 %copy-start = (f32[1,256]{1,0:T(1,128)S(1)}, f32[1,256]{1,0:T(1,128)}, u32[]{:S(2)}) copy-start(f32[1,256]{1,0:T(1,128)} %get-tuple-element.11) | copy-start | bytes 3076

commit v2 on v1

--- a/solution.py
+++ b/solution.py
@@ -81,7 +81,7 @@
     out_ref, misfit_ref,
     lab, src, recv_ref, obs_ref, h, v0, v1, v2, diag, kxo, kxm, kyo, kym, kz,
     czb, qs, up, tall, gat, hot_y, msg, got1, got2, pmsg, pgot, dmsg, dgot, wq, wg, cmsg, cgot, uq, uf,
-    load_sem, h_send, h_recv, q_send, q_recv, ar_send, ar_recv, p_send, p_recv, y_send, y_recv, known,
+    load_sem, h_send, h_recv, g_send, g_recv, q_send, q_recv, ar_send, ar_recv, p_send, p_recv, y_send, y_recv, known,
 ):
     nx, ny = lab.shape[1], lab.shape[2]
     nxc, nyc = nx // 2, ny // 2
@@ -156,13 +156,34 @@
         rows = nx // frames
         return h.at[p, pl.ds(pl.multiple_of(PAD + f * rows, ROWS), rows), :]
 
+    def half(p, which):
+        return h.at[p, pl.ds(PAD + which * (nx // 2), nx // 2), :]
+
+    def thin(p):
+        rows = nx // 2 // frames
+        return h.at[p, pl.ds(pl.multiple_of(PAD + nx // 2 + f * rows, ROWS), rows), :]
+
     copy_cz = send(src.at[0], czb, (q_send, q_recv), 0, (f, slab_at(1)))
     h_sems = (h_send, h_recv)
     odd = lax.rem(s, 2) == 1
     copy_strip = remote(strip(2), strip(6), h_sems, 4, (f, slab_at(-2)))
     copies_strip = [remote(strip(6), strip(6), h_sems, 5 + k, (frame_at(k), s)) for k in range(1, frames)]
     copy_relay = remote(plane(4), plane(6), h_sems, 5, (f, slab_at(-1)))
-    pl.when(odd)(copy_strip.start)
+    even = jnp.logical_not(odd)
+    g_sems = (g_send, g_recv)
+    copy_h0b = remote(half(2, 1), half(0, 1), g_sems, 0, (f, slab_at(1)))
+    copy_h5b = remote(half(3, 1), half(5, 1), g_sems, 0, (f, slab_at(-1)))
+    copy_up = remote(thin(2), thin(0), g_sems, 1, (f, slab_at(1)))
+    copy_down = remote(thin(3), thin(5), g_sems, 1, (f, slab_at(-1)))
+    copies_up = [remote(thin(0), thin(0), g_sems, 1 + k, (frame_at(k), s)) for k in range(1, frames)]
+    copies_down = [remote(thin(5), thin(5), g_sems, 1 + k, (frame_at(k), s)) for k in range(1, frames)]
+
+    @pl.when(odd)
+    def _():
+        copy_up.start()
+        copy_strip.start()
+
+    pl.when(even)(copy_down.start)
     copy_h1 = send(plane(3), plane(1), h_sems, 0, (f, slab_at(1)))
     copy_h4 = send(plane(2), plane(4), h_sems, 1, (f, slab_at(-1)))
 
@@ -182,8 +203,10 @@
     relay_q3 = remote(qs.at[2], qs.at[3], q_sems, 4, (f, slab_at(-1)))
     pl.when(odd)(copy_q3.start)
 
-    copy_h0 = send(plane(2), plane(0), h_sems, 2, (f, slab_at(1)))
-    copy_h5 = send(plane(3), plane(5), h_sems, 3, (f, slab_at(-1)))
+    copy_h0 = send(half(2, 0), half(0, 0), h_sems, 2, (f, slab_at(1)))
+    copy_h5 = send(half(3, 0), half(5, 0), h_sems, 3, (f, slab_at(-1)))
+    pl.when(even)(copy_h0b.start)
+    pl.when(odd)(copy_h5b.start)
     zero_rows = jnp.zeros((PAD, ny), F32)
     for field in (h, v0, v1, v2):
         for p in range(PLANES):
@@ -349,8 +372,17 @@
 
     @pl.when(odd)
     def _():
+        copy_down.wait_recv()
+        for copy in copies_down:
+            copy.start()
         copy_strip.wait_recv()
         for copy in copies_strip:
+            copy.start()
+
+    @pl.when(even)
+    def _():
+        copy_up.wait_recv()
+        for copy in copies_up:
             copy.start()
 
     copy_h1.wait_recv()
@@ -362,16 +394,29 @@
         vertical(e)
     for p in (2, 3):
         coefficients(p)
+    pl.semaphore_wait(known.at[0], heard)
+    heard = tell(known.at[1], quarters, False)
     for copy in copies_q:
         copy.wait_recv()
     pl.when(odd)(relay_q3.start)
     for c in range(3):
         prolong(c)
     m0, m12 = krylov_own()
-    pl.semaphore_wait(known.at[0], heard)
-    heard = tell(known.at[1], quarters, False)
     copy_h0.wait_recv()
     copy_h5.wait_recv()
+
+    @pl.when(odd)
+    def _():
+        copy_h0b.wait_recv()
+        for copy in copies_down:
+            copy.wait()
+
+    @pl.when(even)
+    def _():
+        copy_h5b.wait_recv()
+        for copy in copies_up:
+            copy.wait()
+
     zero_outside(0)
     zero_outside(5)
     vertical(0)
@@ -423,7 +468,6 @@
     mine = jnp.where(inside, misfit([pmsg[j] for j in range(3)]), 0.0)
     dmsg[...] = mine
     dgot[s] = mine
-    share(dmsg, dgot, 1)
     for copy in copies_p:
         copy.wait_recv()
     d = misfit([pmsg[j] + pgot[0, j] + pgot[1, j] + pgot[2, j] for j in range(3)])
@@ -439,6 +483,7 @@
     msg[1] = moments
     got2[s] = moments
     share(msg.at[1], got2, 2)
+    share(dmsg, dgot, 1)
     down = (((1,), (1,)), ((), ()))
     for j, field in enumerate((v0, v1, v2)):
         for t in range(ny // 128):
@@ -483,17 +528,32 @@
         copy.wait_recv()
     u = jnp.concatenate([uf[g, 0] for g in range(frames)], axis=0)
     above = jnp.concatenate([uf[g, 1] for g in range(frames)], axis=0)
-    out_ref[0] = u - jnp.where(s < slabs - 1, above, 0.0)
+    out_ref[0] = u
+    out_ref[1] = jnp.where(s < slabs - 1, above, 0.0)
+
+    @pl.when(odd)
+    def _():
+        for copy in [copy_strip, copy_relay, copy_q3, relay_q3, copy_up, copy_h5b]:
+            copy.wait_send()
+
+    @pl.when(even)
+    def _():
+        copy_down.wait_send()
+        copy_h0b.wait_send()
+
+    for copy in [copy_cz, copy_h0, copy_h1, copy_h4, copy_h5, *copies_q, *copies_p, *copies_w, *copies_c, *copies_u]:
+        copy.wait_send()
+
+
+def difference(u_ref, misfit_in, out_ref, misfit_ref):
+    u = u_ref[0]
+    nxc, nyc = u.shape
+    row_c = lax.broadcasted_iota(jnp.int32, (nxc, nyc), 0)
+    lane_c = lax.broadcasted_iota(jnp.int32, (nxc, nyc), 1)
+    out_ref[0] = u - u_ref[1]
     out_ref[1] = u - jnp.where(row_c < nxc - 1, pltpu.roll(u, nxc - 1, 0), 0.0)
     out_ref[2] = u - jnp.where(lane_c < nyc - 1, pltpu.roll(u, nyc - 1, 1), 0.0)
-
-    @pl.when(odd)
-    def _():
-        for copy in [copy_strip, copy_relay, copy_q3, relay_q3]:
-            copy.wait_send()
-
-    for copy in [copy_cz, copy_h0, copy_h1, copy_h4, copy_h5, *copies_q, *copies_p, *copies_w, *copies_c, *copies_u]:
-        copy.wait_send()
+    misfit_ref[...] = misfit_in[...]
 
 
 def shards(frames, slabs, labels, region_conductivity, source, receivers, observed):
@@ -533,6 +593,7 @@
         pltpu.VMEM((frames, 2, quarter, nyc), F32),
         pltpu.SemaphoreType.DMA((4,)),
         *[pltpu.SemaphoreType.DMA((5 + frames,)) for _ in range(2)],
+        *[pltpu.SemaphoreType.DMA((1 + frames,)) for _ in range(2)],
         *[pltpu.SemaphoreType.DMA((5,)) for _ in range(2)],
         *[pltpu.SemaphoreType.DMA((3,)) for _ in range(2)],
         *[pltpu.SemaphoreType.DMA((3,)) for _ in range(2)],
@@ -541,7 +602,7 @@
     ]
     out, misfit = pl.pallas_call(
         functools.partial(kernel, frames, slabs, region_conductivity.shape[0]),
-        out_shape=(jax.ShapeDtypeStruct((3, nxc, nyc), F32), jax.ShapeDtypeStruct((1, recv), F32)),
+        out_shape=(jax.ShapeDtypeStruct((2, nxc, nyc), F32), jax.ShapeDtypeStruct((1, recv), F32)),
         in_specs=[hbm, pl.BlockSpec(memory_space=pltpu.SMEM), hbm, hbm, hbm],
         out_specs=(vmem, vmem),
         scratch_shapes=scratch,
@@ -549,6 +610,12 @@
             collective_id=0, has_side_effects=True, vmem_limit_bytes=64 * 1024 * 1024
         ),
     )(labels, region_conductivity, source, jnp.transpose(receivers, (1, 0, 2)), observed)
+    out, misfit = pl.pallas_call(
+        difference,
+        out_shape=(jax.ShapeDtypeStruct((3, nxc, nyc), F32), jax.ShapeDtypeStruct((1, recv), F32)),
+        in_specs=[vmem, vmem],
+        out_specs=(vmem, vmem),
+    )(out, misfit)
     return out.reshape(1, 3, 1, nxc, nyc), misfit
 
 

time: 51.1 us -> 48.5 us (0.949); the launches traced: 50.1 us -> 48.3 us
  local copies, waits for them, and re-layouts: 2.18 us -> 0 us
    unnamed x4 -> x0, local copies, waits for them, and re-layouts: 2.18 us -> none
    pallas_call x0 -> x1, Pallas kernels: none -> 1.67 us  [shards(): pl.pallas_call(difference, out_shape=(jax.ShapeDtypeStruct((3, nxc, nyc),...]
    pallas_call x1, Pallas kernels: 47.3 us -> 46 us  [shards(): pl.pallas_call(functools.partial(kernel, frames, slabs, region_conductivi...]
where the time goes in v2:
time: 48.5 us; the launch traced here: 48.3 us
  Pallas kernels  47.7 us (98%)
  between operations  0.64 us (1%)
    pallas_call x1, Pallas kernels, shards(): pl.pallas_call(functools.partial(kernel, frames, slabs, region_conductivi...  46 us
    pallas_call x1, Pallas kernels, shards(): pl.pallas_call(difference, out_shape=(jax.ShapeDtypeStruct((3, nxc, nyc),...  1.67 us

profile of v2, /device:TPU:1, one launch (start us, length us, event | category | flops | bytes accessed | tf_op | source)
XLA Modules:
  0.0 48.3 jit_solution(9673321506048268048)
XLA Ops:
  0.6 46.0 %shard_map.68 = (f32[2,64,256]{2,1,0:T(8,128)}, f32[1,256]{1,0:T(1,128)}) custom-call(s32[2,128,512]{2,1,0:T(8,128)} %labels_ref.1, f32[8]{0:T(128)} %cond_ref.1, f32[1,3,1,64,256]{4,3,2,1,0:T(8,128)} %source_ref.1, s32[3,1,256]{2,1,0:T(1,128)} %bitcast.4, f32[1,256]{1,0:T(1,128)} %obs_hbm.1), custom_call_target="tpu_custom_call" | custom-call | tf_op jit(solution)/shard_map/pallas_call | solution.py:603
  46.7 1.7 %shard_map.69 = (f32[3,64,256]{2,1,0:T(8,128)}, f32[1,256]{1,0:T(1,128)}) custom-call(f32[2,64,256]{2,1,0:T(8,128)} %get-tuple-element.6.u_ref, f32[1,256]{1,0:T(1,128)} %get-tuple-element.7.misfit_in), custom_call_target="tpu_custom_call" | custom-call | tf_op jit(solution)/shard_map/pallas_call | solution.py:613

commit v3 on v2

--- a/solution.py
+++ b/solution.py
@@ -363,8 +363,8 @@
             src_ref=others, dst_ref=others, send_sem=ar_send.at[index], recv_sem=ar_recv.at[index],
             device_id=(f, slab_at(1)), device_id_type=MESH,
         )
-        whole.wait_send()
         whole.wait_recv()
+        return whole
 
     def moments_of(landing):
         total = jnp.sum(landing[...], axis=0)
@@ -458,7 +458,7 @@
         send(pmsg, pgot.at[1], p_sems, 1, (f, slab_at(-1))),
         send(pmsg, pgot.at[2], p_sems, 2, (f, slab_at(-2))),
     ]
-    shared(got1, 0)
+    sent1 = shared(got1, 0)
     c0, c1, c2 = cg_coefficients(moments_of(got1))
     observed = obs_ref[...]
 
@@ -483,7 +483,6 @@
     msg[1] = moments
     got2[s] = moments
     share(msg.at[1], got2, 2)
-    share(dmsg, dgot, 1)
     down = (((1,), (1,)), ((), ()))
     for j, field in enumerate((v0, v1, v2)):
         for t in range(ny // 128):
@@ -502,7 +501,8 @@
         to = frame_at(k)
         copies_w.append(send(wq.at[to], wg.at[1, f], y_sems, k, (to, slab_at(-1))))
         copies_w.append(send(wq.at[to], wg.at[0, f], y_sems, frames + k, (to, s)))
-    shared(got2, 2)
+    share(dmsg, dgot, 1)
+    sent2 = shared(got2, 2)
     place = lax.broadcasted_iota(jnp.int32, (1, 128), 1)
     c_row = jnp.zeros((1, 128), F32)
     for j, c in enumerate(cg_coefficients(moments_of(got2))):
@@ -522,7 +522,7 @@
             uq[g, side] = sum(float(inverse[g, k]) * w[k] for k in range(frames))
     uf[f] = uq[f]
     copies_u = [send(uq.at[frame_at(k)], uf.at[f], y_sems, 3 * frames + k, (frame_at(k), s)) for k in range(1, frames)]
-    shared(dgot, 1)
+    sent3 = shared(dgot, 1)
     misfit_ref[...] = jnp.sum(dgot[...], axis=0)
     for copy in copies_u:
         copy.wait_recv()
@@ -541,7 +541,7 @@
         copy_down.wait_send()
         copy_h0b.wait_send()
 
-    for copy in [copy_cz, copy_h0, copy_h1, copy_h4, copy_h5, *copies_q, *copies_p, *copies_w, *copies_c, *copies_u]:
+    for copy in [copy_cz, copy_h0, copy_h1, copy_h4, copy_h5, *copies_q, *copies_p, *copies_w, *copies_c, *copies_u, sent1, sent2, sent3]:
         copy.wait_send()
 
 

time: 48.5 us -> 48.2 us (level); the launches traced: 48.3 us -> 47.4 us
  Pallas kernels: 47.7 us -> 46.8 us
    pallas_call x1, Pallas kernels: 46 us -> 45.1 us  [shards(): pl.pallas_call(functools.partial(kernel, frames, slabs, region_conductivi...]
where the time goes in v3:
time: 48.2 us; the launch traced here: 47.4 us
  Pallas kernels  46.8 us (97%)
  between operations  0.64 us (1%)
    pallas_call x1, Pallas kernels, shards(): pl.pallas_call(functools.partial(kernel, frames, slabs, region_conductivi...  45.1 us
    pallas_call x1, Pallas kernels, shards(): pl.pallas_call(difference, out_shape=(jax.ShapeDtypeStruct((3, nxc, nyc),...  1.67 us

profile of v3, /device:TPU:1, one launch (start us, length us, event | category | flops | bytes accessed | tf_op | source)
XLA Modules:
  0.0 47.4 jit_solution(1434812348914197781)
XLA Ops:
  0.6 45.1 %shard_map.68 = (f32[2,64,256]{2,1,0:T(8,128)}, f32[1,256]{1,0:T(1,128)}) custom-call(s32[2,128,512]{2,1,0:T(8,128)} %labels_ref.1, f32[8]{0:T(128)} %cond_ref.1, f32[1,3,1,64,256]{4,3,2,1,0:T(8,128)} %source_ref.1, s32[3,1,256]{2,1,0:T(1,128)} %bitcast.4, f32[1,256]{1,0:T(1,128)} %obs_hbm.1), custom_call_target="tpu_custom_call" | custom-call | tf_op jit(solution)/shard_map/pallas_call | solution.py:603
  45.7 1.7 %shard_map.69 = (f32[3,64,256]{2,1,0:T(8,128)}, f32[1,256]{1,0:T(1,128)}) custom-call(f32[2,64,256]{2,1,0:T(8,128)} %get-tuple-element.6.u_ref, f32[1,256]{1,0:T(1,128)} %get-tuple-element.7.misfit_in), custom_call_target="tpu_custom_call" | custom-call | tf_op jit(solution)/shard_map/pallas_call | solution.py:613
